TPU v7x, 32 devices: a whole 2x2x4 slice. The times are simulated.
32 devices in a mesh: groups: 2 (over y), leaf: 8 (over z, x), sub: 2 (over core).
Axes of the slice: x: 2, y: 2, z: 4, core: 2. Of those that a mesh axis runs over, the one named last changes fastest.
Arguments:
- vectors: float32 [32, 32768], P('sub', ('groups', 'leaf')), parts along dimension 1, may hold values from -6 to 6
- points: float32 [3, 32768], P(None, ('groups', 'leaf')), parts along dimension 1, may hold values from 0 to 1
- leaf_basis: float32 [256, 64, 128], P(('groups', 'leaf')), parts along dimension 0, may hold values from -0.5 to 0.5
- local_transfer: float32 [496, 64, 64], P(('groups', 'leaf')), parts along dimension 0, may hold values from -0.5 to 0.5
- local_skeleton: float32 [480, 3, 64], P(('groups', 'leaf')), parts along dimension 0, may hold values from 0 to 1
- upper_transfer: float32 [6, 64, 64], replicated, may hold values from -0.5 to 0.5
- upper_skeleton: float32 [15, 3, 64], replicated, may hold values from 0 to 1
- near_list: int32 [2, 8192], P(None, ('groups', 'leaf')), parts along dimension 1, may hold values from 0 to 47, as said below
- far_list: int32 [2, 2048], P(None, ('groups', 'leaf')), parts along dimension 1, may hold values from 0 to 89, as said below
- upper_list: int32 [2, 256], P(None, ('groups', 'leaf')), parts along dimension 1, may hold values from 0 to 13, as said below
Outputs:
- product: float32 [32, 32768], P('sub', ('groups', 'leaf')), parts along dimension 1
There are 2 independent parts, one for each index of `groups`. A program takes and returns all parts, laid end to end along the dimension named above; an argument that names none is the same for every part. Nothing has to cross between parts.
Inputs may be any that keep to these rules, and one draw needn't show every extreme that they name: near_list[0] is a leaf of the owner, 0 to 15; near_list[1] counts leaves from the first leaf of the previous owner, 0 to 47. far_list[0] is a node of the owner below its root; far_list[1] counts nodes below the roots of owners o - 1, o, o + 1 in a row, and names a node of the same level as the row node. `upper_list`: both nodes of a pair are of the same level, never the root; an owner's pairs may name any upper nodes.
All inputs are finite; a program needn't handle non-finite values.
Results may differ from a plain program's by a relative error of at most 0.0003.
Values sent between devices are 32-bit elements; how exact they have to be, the bound alone decides.
A program may use at most 128 MiB of HBM per device.

v0:
```python
import functools
import math

import jax
import jax.numpy as jnp
from jax import lax
from jax.experimental import pallas as pl
from jax.experimental.pallas import tpu as pltpu
from jax.sharding import PartitionSpec as P

root_three = math.sqrt(3.0)
length_scale = 0.3
log2e = math.log2(math.e)
ln2 = math.log(2.0)
point_scale = root_three / length_scale * log2e
highest = lax.Precision.HIGHEST
MESH = pl.DeviceIdType.MESH
FEATURES = 32
GROUP = 16
FAR_GROUP = 16
f32 = jnp.float32
bf16 = jnp.bfloat16


def level_table(count):
    offsets = []
    counts = []
    anchor = 0
    extent = count
    while extent >= 1:
        offsets.append(anchor)
        counts.append(extent)
        anchor += extent
        extent //= 2
    return (offsets, counts)


def dot_nt(a, b):
    return lax.dot_general(
        a, b, (((1,), (1,)), ((), ())), precision=highest, preferred_element_type=f32
    )


def dot_nn(a, b):
    return lax.dot_general(
        a, b, (((1,), (0,)), ((), ())), precision=highest, preferred_element_type=f32
    )


def dot_fast(a, b):
    return lax.dot_general(a, b, (((1,), (0,)), ((), ())), preferred_element_type=f32)


def each(start, stop, body):
    if stop - start <= 16:
        for i in range(start, stop):
            body(i)
    else:

        @pl.loop(start, stop)
        def _(i):
            body(i)


def split(values):
    high = values.astype(bf16)
    return high, (values - high.astype(f32)).astype(bf16)


def kernel_values(squared):
    squared = jnp.maximum(squared, 1e-20)
    t = squared * lax.rsqrt(squared)
    return (t + log2e) * jnp.exp2(-t)


def product(values, kernel):
    kernel_high, kernel_low = split(kernel)
    high, low = split(values)
    rows = values.shape[0]
    both = dot_fast(jnp.concatenate([high, low], axis=0), kernel_high)
    return both[:rows] + both[rows:] + dot_fast(high, kernel_low)


def features(p):
    q = (p - 0.5) * point_scale
    high = q.astype(bf16).astype(f32)
    low = (q - high).astype(bf16).astype(f32)
    q = high + low
    norm = jnp.sum(q * q, axis=0, keepdims=True)
    n1 = norm.astype(bf16).astype(f32)
    n2 = (norm - n1).astype(bf16).astype(f32)
    n3 = norm - n1 - n2
    return high, low, n1, n2, n3


def put_features(feat, p, width):
    high, low, n1, n2, n3 = features(p)
    span = slice(0, width)
    one = jnp.ones((1, width), f32)
    for k, rows in enumerate((high, low, high, low)):
        feat[0, 3 * k : 3 * k + 3, span] = -2.0 * rows
    for k, rows in enumerate((high, high, low, low)):
        feat[1, 3 * k : 3 * k + 3, span] = rows
    for k, rows in enumerate((n1, n2, n3, one, one, one)):
        feat[0, 12 + k : 13 + k, span] = rows
    for k, rows in enumerate((one, one, one, n1, n2, n3)):
        feat[1, 12 + k : 13 + k, span] = rows


def exchange_kernel(
    n,
    halo_width,
    x_ref,
    pts_ref,
    basis_ref,
    tr_ref,
    ulist_ref,
    nlist_ref,
    xall,
    ptsall,
    packed,
    roots,
    cols_out,
    wts_out,
    own_out,
    halo_send,
    halo_recv,
    root_send,
    root_recv,
    call,
    feat,
    near_t,
    near_row,
    spread,
):
    me = lax.axis_index("leaf")
    leaf_count, rank, leaf = basis_ref.shape
    vecs = x_ref.shape[0]
    lower = 2 * leaf_count - 2
    offsets, counts = level_table(leaf_count)
    entries = ulist_ref.shape[1]

    barrier = pltpu.get_barrier_semaphore()

    def greet(d):
        pl.semaphore_signal(
            barrier, inc=1, device_id={"leaf": lax.rem(me + d, n)}, device_id_type=MESH
        )

    each(1, n, greet)
    pl.semaphore_wait(barrier, n - 1)

    own_pts = pts_ref.at[:, pl.ds(0, halo_width)]
    own_coefs = packed.at[1]
    sources = (x_ref, own_pts, own_coefs)

    def halo(kind, side):
        slot = 2 * side
        target = (xall.at[slot], ptsall.at[slot], packed.at[slot])[kind]
        other = jnp.minimum(me + 1, n - 1) if side == 0 else jnp.maximum(me - 1, 0)
        return pltpu.make_async_remote_copy(
            src_ref=sources[kind],
            dst_ref=target,
            send_sem=halo_send.at[kind, side],
            recv_sem=halo_recv.at[kind, side],
            device_id={"leaf": other},
            device_id_type=MESH,
        )

    def sends(side):
        return me < n - 1 if side == 0 else me > 0

    def receives(side):
        return me > 0 if side == 0 else me < n - 1

    for side in range(2):

        @pl.when(sends(side))
        def _():
            halo(0, side).start()
            halo(1, side).start()

    def up(node):
        return dot_nt(call[node], tr_ref[node])

    def keep(node, value):
        call[node] = value
        half = node % 2 * rank
        packed[1, node // 2, :, half : half + rank] = value

    for i in range(leaf_count):
        keep(i, dot_nt(x_ref[:, i * leaf : (i + 1) * leaf], basis_ref[i]))
    for height in range(1, len(counts) - 1):
        below = offsets[height - 1]
        for j in range(counts[height]):
            keep(offsets[height] + j, up(below + 2 * j) + up(below + 2 * j + 1))
    for side in range(2):

        @pl.when(sends(side))
        def _():
            halo(2, side).start()

    root = up(lower - 2) + up(lower - 1)
    roots[me] = jnp.zeros(roots.shape[1:], f32)
    roots[me, 0:vecs, 0:rank] = root
    roots[me, 0:vecs, rank : 2 * rank] = dot_nt(root, tr_ref[lower])
    roots[me, vecs : vecs + 2, 0:entries] = ulist_ref[...].astype(f32)

    def root_copy(d):
        return pltpu.make_async_remote_copy(
            src_ref=roots.at[me],
            dst_ref=roots.at[me],
            send_sem=root_send.at[d],
            recv_sem=root_recv.at[d],
            device_id={"leaf": lax.rem(me + d, n)},
            device_id_type=MESH,
        )

    def root_arrival(d):
        sender = lax.rem(me + n - d, n)
        return pltpu.make_async_remote_copy(
            src_ref=roots.at[me],
            dst_ref=roots.at[sender],
            send_sem=root_send.at[d],
            recv_sem=root_recv.at[d],
            device_id={"leaf": lax.rem(me + d, n)},
            device_id_type=MESH,
        )

    each(1, n, lambda d: root_copy(d).start())

    xall[1] = x_ref[...]
    ptsall[1] = pts_ref[:, 0:halo_width]
    for side in range(2):
        slot = 2 * side

        @pl.when(jnp.logical_not(receives(side)))
        def _():
            xall[slot] = jnp.zeros(xall.shape[1:], f32)
            ptsall[slot] = jnp.zeros(ptsall.shape[1:], f32)
            packed[slot] = jnp.zeros(packed.shape[1:], f32)

    total = nlist_ref.shape[1]
    row_hot = (
        lax.broadcasted_iota(jnp.int32, (leaf_count, total), 0) == nlist_ref[0:1, :]
    ).astype(f32).astype(bf16)
    col_hot = (
        lax.broadcasted_iota(jnp.int32, (128, total), 0) == nlist_ref[1:2, :]
    ).astype(f32).astype(bf16)
    count = lax.dot_general(
        row_hot, col_hot, (((1,), (1,)), ((), ())), preferred_element_type=f32
    )
    col_id = lax.broadcasted_iota(jnp.int32, count.shape, 1)
    own = jnp.logical_and(col_id >= leaf_count, col_id < 2 * leaf_count)
    has = jnp.where(jnp.logical_or(own, count < 0.5), 0.0, 1.0)
    before = (
        lax.broadcasted_iota(jnp.int32, (128, 128), 0)
        < lax.broadcasted_iota(jnp.int32, (128, 128), 1)
    ).astype(f32).astype(bf16)
    place = dot_fast(has.astype(bf16), before)
    place = jnp.where(has > 0.5, place, -1.0)
    lane = lax.broadcasted_iota(jnp.int32, (leaf_count, 128), 1)
    lane_f = lane.astype(f32)
    cols = jnp.zeros((leaf_count, 128), f32)
    wts = jnp.zeros((leaf_count, 128), f32)
    for c in [*range(leaf_count), *range(2 * leaf_count, 3 * leaf_count)]:
        hit = place[:, c : c + 1] == lane_f
        cols = cols + jnp.where(hit, float(c), 0.0)
        wts = wts + jnp.where(hit, count[:, c : c + 1], 0.0)
    filled = jnp.sum(has, axis=1, keepdims=True)
    cols_out[...] = jnp.where(lane == 127, filled, cols).astype(jnp.int32)
    wts_out[...] = wts * ln2

    npts = leaf_count * leaf
    put_features(feat, pts_ref[:, 0:npts], npts)
    feat[:, 18:FEATURES, :] = jnp.zeros((2, FEATURES - 18, npts), f32)
    near_row[...] = feat[1].astype(bf16)
    for i in range(leaf_count):
        near_t[i * leaf : (i + 1) * leaf, :] = feat[0, :, i * leaf : (i + 1) * leaf].T.astype(bf16)
    leaf_of = lax.broadcasted_iota(jnp.int32, (128, npts), 1) // leaf + leaf_count
    chosen = (leaf_of == lax.broadcasted_iota(jnp.int32, (128, npts), 0)).astype(f32)
    spread[...] = dot_nn(count * ln2, chosen)

    @pl.loop(0, leaf_count)
    def _(r):
        lanes = pl.ds(pl.multiple_of(r * leaf, leaf), leaf)
        kernel = kernel_values(dot_fast(near_t[...], near_row[:, lanes]))
        own_out[:, lanes] = product(x_ref[...] * spread[pl.ds(r, 1), :], kernel)

    for side in range(2):

        @pl.when(sends(side))
        def _():
            for kind in range(3):
                halo(kind, side).wait_send()

        @pl.when(receives(side))
        def _():
            for kind in range(3):
                halo(kind, side).wait_recv()

    def finish(d):
        root_copy(d).wait_send()
        root_arrival(d).wait_recv()

    each(1, n, finish)


def couple_kernel(
    n,
    entries,
    cols_ref,
    wts_ref,
    far_ref,
    xall,
    ptsall,
    uppts_ref,
    packed,
    roots,
    basis_ref,
    tr_ref,
    uptr_ref,
    own_ref,
    out_ref,
    feat,
    near_t,
    near_row,
    skel_t,
    skel_row,
    up_t,
    up_row,
    y_ref,
    upc,
    call,
):
    me = lax.axis_index("leaf")
    leaf_count, rank, leaf = basis_ref.shape
    vecs = out_ref.shape[0]
    lower = 2 * leaf_count - 2
    npts = leaf_count * leaf
    nskel = lower * rank
    offsets, counts = level_table(leaf_count)
    up_offsets, up_counts = level_table(n)

    put = functools.partial(put_features, feat)

    def columns_to(target, first, start, width):
        for t in range(width // 128):
            tile = feat[0, :, start + t * 128 : start + (t + 1) * 128]
            target[first + t * 128 : first + (t + 1) * 128, :] = tile.T.astype(bf16)

    feat[...] = jnp.zeros(feat.shape, f32)
    for slot in range(3):
        put(ptsall[slot], npts + nskel)
        columns_to(near_t, slot * npts, 0, npts)
        columns_to(skel_t, slot * nskel, npts, nskel)
        if slot == 1:
            near_row[...] = feat[1, :, 0:npts].astype(bf16)
            skel_row[...] = jnp.zeros(skel_row.shape, bf16)
            for j in range(lower):
                tile = feat[1, :, npts + j * rank : npts + (j + 1) * rank].astype(bf16)
                for h in range(2):
                    skel_row[2 * j + h, :, h * rank : (h + 1) * rank] = tile

    chunk = math.gcd(uppts_ref.shape[1], 1024)

    def up_chunk(i):
        base = i * chunk if isinstance(i, int) else pl.multiple_of(i * chunk, chunk)
        put(uppts_ref[:, pl.ds(base, chunk)], chunk)
        for t in range(chunk // 128):
            tile = feat[0, :, t * 128 : (t + 1) * 128]
            up_t[pl.ds(base + t * 128, 128), :] = tile.T.astype(bf16)
        for j in range(chunk // rank):
            up_row[i * (chunk // rank) + j] = feat[1, :, j * rank : (j + 1) * rank].astype(bf16)

    each(0, uppts_ref.shape[1] // chunk, up_chunk)

    def load_roots(j):
        upc[j] = roots[j, 0:vecs, 0:rank]

    each(0, n, load_roots)

    def first_lift(j):
        upc[n + j] = roots[2 * j, 0:vecs, rank : 2 * rank] + roots[2 * j + 1, 0:vecs, rank : 2 * rank]

    each(0, n // 2, first_lift)
    for height in range(2, len(up_counts)):

        def lift(j, height=height):
            child = up_offsets[height - 1] + 2 * j
            upc[up_offsets[height] + j] = dot_nt(upc[child], uptr_ref[child - n]) + dot_nt(
                upc[child + 1], uptr_ref[child + 1 - n]
            )

        each(0, up_counts[height], lift)

    pair_rows = roots[:, vecs, :]
    pair_cols = roots[:, vecs + 1, :]
    used = lax.broadcasted_iota(jnp.int32, pair_rows.shape, 1) < entries
    value = None
    for height in range(len(up_counts) - 1, -1, -1):
        node = up_offsets[height] + lax.div(me, 2**height)
        mine = jnp.logical_and(pair_rows == node.astype(f32), used)
        row_feat = up_row[node]

        def term(c, mine=mine, row_feat=row_feat):
            named = jnp.logical_and(mine, pair_cols == jnp.asarray(c, f32))
            times = jnp.sum(jnp.sum(jnp.where(named, ln2, 0.0), axis=1, keepdims=True), axis=0, keepdims=True)
            start = c * rank if isinstance(c, int) else pl.multiple_of(c * rank, rank)
            kernel = kernel_values(dot_fast(up_t[pl.ds(start, rank), :], row_feat))
            return product(upc[c] * times, kernel)

        first = up_offsets[height]
        if up_counts[height] <= 16:
            level = sum(term(first + j) for j in range(up_counts[height]))
        else:
            level = lax.fori_loop(
                0,
                up_counts[height],
                lambda j, acc: acc + term(first + j),
                jnp.zeros((vecs, rank), f32),
            )
        if value is not None:
            if height == 0:
                level = level + dot_nn(value, tr_ref[lower])
            else:
                level = level + dot_nn(value, uptr_ref[node - n])
        value = level

    y_ref[...] = jnp.zeros(y_ref.shape, f32)
    y_ref[lower] = value * (1.0 / ln2)

    for slot in range(3):
        for j in range(lower):
            half = j % 2 * rank
            call[slot * lower + j] = packed[slot, j // 2, :, half : half + rank]
    far_total = far_ref.shape[1]
    far_group = math.gcd(far_total, FAR_GROUP)

    @pl.loop(0, far_total // far_group)
    def _(g):
        named = [
            (far_ref[0, g * far_group + k], far_ref[1, g * far_group + k]) for k in range(far_group)
        ]
        tiles = []
        for k in range(0, far_group, 2):
            tiles.append(
                sum(
                    dot_fast(
                        skel_t[pl.ds(pl.multiple_of(named[k + h][1] * rank, rank), rank), :],
                        skel_row[2 * named[k + h][0] + h],
                    )
                    for h in range(2)
                )
            )
        kernel_high, kernel_low = split(kernel_values(jnp.concatenate(tiles, axis=0)))
        parts = []
        for k in range(0, far_group, 2):
            rows = slice(k // 2 * rank, (k // 2 + 1) * rank)
            high, low = split(
                jnp.concatenate([call[named[k][1]], call[named[k + 1][1]]], axis=0)
            )
            both = dot_fast(jnp.concatenate([high, low], axis=0), kernel_high[rows])
            parts.append(
                both[: 2 * vecs] + both[2 * vecs :] + dot_fast(high, kernel_low[rows])
            )
        for k in range(far_group):
            h = k % 2
            y_ref[named[k][0]] += parts[k // 2][h * vecs : (h + 1) * vecs, h * rank : (h + 1) * rank]

    for height in range(len(counts) - 2, -1, -1):
        for j in range(counts[height]):
            node = offsets[height] + j
            y_ref[node] += dot_nn(y_ref[offsets[height + 1] + j // 2], tr_ref[node])

    for i in range(leaf_count):
        span = slice(i * leaf, (i + 1) * leaf)
        out_ref[:, span] = own_ref[:, span] + dot_nn(y_ref[i] * ln2, basis_ref[i])

    @pl.loop(0, leaf_count)
    def _(r):
        lanes = pl.ds(pl.multiple_of(r * leaf, leaf), leaf)
        row_feat = near_row[:, lanes]
        filled = cols_ref[r, 127]
        wide = lax.div(filled + (GROUP // 2 - 1), GROUP)
        narrow = lax.div(jnp.maximum(filled - wide * GROUP, 0) + (GROUP // 2 - 1), GROUP // 2)

        def near_group(first, size, acc):
            values = []
            places = []
            for k in range(size):
                c = cols_ref[r, first + k]
                slot = lax.div(c, leaf_count)
                inside = pl.multiple_of((c - slot * leaf_count) * leaf, leaf)
                values.append(xall[slot, :, pl.ds(inside, leaf)] * wts_ref[r, first + k])
                places.append(near_t[pl.ds(pl.multiple_of(c * leaf, leaf), leaf), :])
            kernel = kernel_values(dot_fast(jnp.concatenate(places, axis=0), row_feat))
            return acc + product(jnp.concatenate(values, axis=1), kernel)

        acc = lax.fori_loop(
            0, wide, lambda g, acc: near_group(g * GROUP, GROUP, acc), out_ref[:, lanes]
        )
        acc = lax.fori_loop(
            0, narrow, lambda g, acc: near_group(wide * GROUP, GROUP // 2, acc), acc
        )
        out_ref[:, lanes] = acc


def per_device(
    vectors,
    points,
    leaf_basis,
    local_transfer,
    local_skeleton,
    upper_transfer,
    upper_skeleton,
    near_list,
    far_list,
    upper_list,
):
    leaf_count, rank, leaf = leaf_basis.shape
    vecs, npts = vectors.shape
    n = lax.axis_size("leaf")
    lower = 2 * leaf_count - 2
    nskel = lower * rank
    halo_width = npts + nskel
    nup = 2 * n * rank
    vmem = pl.BlockSpec(memory_space=pltpu.VMEM)
    smem = pl.BlockSpec(memory_space=pltpu.SMEM)
    pts = jnp.concatenate(
        [points, jnp.transpose(local_skeleton, (1, 0, 2)).reshape(3, nskel)], axis=1
    )
    uppts = jnp.pad(
        jnp.transpose(upper_skeleton, (1, 0, 2)).reshape(3, (2 * n - 1) * rank), ((0, 0), (0, rank))
    )
    root_rows = vecs + 8
    xall, ptsall, packed, roots, cols, wts, near_own = pl.pallas_call(
        functools.partial(exchange_kernel, n, halo_width),
        out_shape=(
            jax.ShapeDtypeStruct((3, vecs, npts), f32),
            jax.ShapeDtypeStruct((3, 3, halo_width), f32),
            jax.ShapeDtypeStruct((3, lower // 2, vecs, 2 * rank), f32),
            jax.ShapeDtypeStruct((n, root_rows, 2 * rank), f32),
            jax.ShapeDtypeStruct((leaf_count, 128), jnp.int32),
            jax.ShapeDtypeStruct((leaf_count, 128), f32),
            jax.ShapeDtypeStruct((vecs, npts), f32),
        ),
        in_specs=[vmem] * 6,
        out_specs=(vmem,) * 7,
        scratch_shapes=[
            pltpu.SemaphoreType.DMA((3, 2)),
            pltpu.SemaphoreType.DMA((3, 2)),
            pltpu.SemaphoreType.DMA((n,)),
            pltpu.SemaphoreType.DMA((n,)),
            pltpu.VMEM((lower, vecs, rank), f32),
            pltpu.VMEM((2, FEATURES, npts), f32),
            pltpu.VMEM((npts, FEATURES), bf16),
            pltpu.VMEM((FEATURES, npts), bf16),
            pltpu.VMEM((leaf_count, npts), f32),
        ],
        compiler_params=pltpu.CompilerParams(
            collective_id=0, has_side_effects=True, vmem_limit_bytes=40 * 2**20
        ),
    )(vectors, pts, leaf_basis, local_transfer, upper_list, near_list)
    return pl.pallas_call(
        functools.partial(couple_kernel, n, upper_list.shape[1]),
        out_shape=jax.ShapeDtypeStruct((vecs, npts), f32),
        in_specs=[smem] * 3 + [vmem] * 9,
        out_specs=vmem,
        scratch_shapes=[
            pltpu.VMEM((2, FEATURES, halo_width), f32),
            pltpu.VMEM((3 * npts, FEATURES), bf16),
            pltpu.VMEM((FEATURES, npts), bf16),
            pltpu.VMEM((3 * nskel, FEATURES), bf16),
            pltpu.VMEM((2 * lower, FEATURES, 2 * rank), bf16),
            pltpu.VMEM((nup, FEATURES), bf16),
            pltpu.VMEM((2 * n, FEATURES, rank), bf16),
            pltpu.VMEM((lower + 1, vecs, rank), f32),
            pltpu.VMEM((2 * n, vecs, rank), f32),
            pltpu.VMEM((3 * lower, vecs, rank), f32),
        ],
        compiler_params=pltpu.CompilerParams(vmem_limit_bytes=48 * 2**20),
    )(cols, wts, far_list, xall, ptsall, uppts, packed, roots, leaf_basis, local_transfer, upper_transfer, near_own)


def solution(mesh):
    return jax.shard_map(
        per_device,
        mesh=mesh,
        in_specs=(
            P("sub", ("groups", "leaf")),
            P(None, ("groups", "leaf")),
            P(("groups", "leaf"), None, None),
            P(("groups", "leaf"), None, None),
            P(("groups", "leaf"), None, None),
            P(),
            P(),
            P(None, ("groups", "leaf")),
            P(None, ("groups", "leaf")),
            P(None, ("groups", "leaf")),
        ),
        out_specs=P("sub", ("groups", "leaf")),
        check_vma=False,
    )
```

profile of v0, /device:TPU:4, one launch (start us, length us, event | category | flops | bytes accessed | tf_op | source)
XLA Modules:
  0.0 50.0 jit_solution(7850535952777487544)
XLA Ops:
  0.0 0.0 copy-start.9
  0.0 0.0 copy-start.10
  0.0 0.0 copy-start.5
  0.0 0.9 %reshape.7 = f32[3,960]{1,0:T(4,128)S(1)} reshape(f32[3,15,64]{2,1,0:T(8,128)} %bitcast.3) | data formatting | bytes 23040 | tf_op jit(solution)/shard_map/reshape | solution.py:534
  0.9 0.0 copy-done.9
  0.9 0.1 reshape.6
  1.0 0.0 copy-done.10
  1.0 0.0 copy-start.6
  1.0 0.0 copy-start.8
  1.0 0.0 copy-done.5
  1.0 0.6 %copy-done.6 = s32[2,512]{1,0:T(2,128)S(1)} copy-done((s32[2,512]{1,0:T(2,128)S(1)}, s32[2,512]{1,0:T(2,128)}, u32[]{:S(2)}) %copy-start.6) | copy-done | bytes 4120
  1.7 0.0 copy-done.8
  1.7 0.0 copy-start
  1.7 1.2 %copy-done = f32[31,64,64]{2,1,0:T(8,128)S(1)} copy-done((f32[31,64,64]{2,1,0:T(8,128)S(1)}, f32[31,64,64]{2,1,0:T(8,128)}, u32[]{:S(2)}) %copy-start) | copy-done | bytes 507928
  2.9 0.0 copy-start.2
  2.9 1.0 %copy-done.2 = f32[16,64,128]{2,1,0:T(8,128)S(1)} copy-done((f32[16,64,128]{2,1,0:T(8,128)S(1)}, f32[16,64,128]{2,1,0:T(8,128)}, u32[]{:S(2)}) %copy-start.2) | copy-done | bytes 524312
  3.9 0.0 copy-start.1
  3.9 0.0 copy-start.3
  3.9 0.0 copy-start.4
  3.9 20.0 %shard_map.100 = (f32[3,16,2048]{2,1,0:T(8,128)S(1)}, f32[3,3,3968]{2,1,0:T(4,128)S(1)}, f32[3,15,16,128]{3,2,1,0:T(8,128)S(1)}, f32[8,24,128]{2,1,0:T(8,128)S(1...) custom-call(f32[16,2048]{1,0:T(8,128)S(1)} %copy-done.5, ...), custom_call_target="tpu_custom_call" | custom-call | tf_op jit(solution)/shard_map/pallas_call | solution.py:537
  24.0 0.0 copy-start.7
  24.0 0.0 copy-done.1
  24.0 0.0 copy-done.3
  24.0 0.0 copy-done.4
  24.0 0.6 %copy-done.7 = s32[2,128]{1,0:T(2,128)S(1)} copy-done((s32[2,128]{1,0:T(2,128)S(1)}, s32[2,128]{1,0:T(2,128)}, u32[]{:S(2)}) %copy-start.7) | copy-done | bytes 1048
  24.7 25.4 %shard_map.101 = f32[16,2048]{1,0:T(8,128)} custom-call(s32[16,128]{1,0:T(8,128)S(1)} %get-tuple-element.12.cols_ref, f32[16,128]{1,0:T(8,128)S(1)} %get-tuple-element.13.wts_ref, s32[2,128]{1,0:T(2,128)S(1)} %copy-done.7, f32[3,16,2048]{2,1,0:T(8,128)S(1)} %get-tuple-element.14.xall, f32[3,3,3968]{2,1,0:T(4,128)S(1)} %get-tuple-element.15.ptsall, ...), custom_call_target="tpu_custom_call" | custom-call | tf_op jit(solution)/shard_map/pallas_call | solution.py:565
  (2 shorter events, 0.0 us)
Async XLA Ops:
  0.0 0.9 %copy-start.9 = (f32[30,3,64]{2,0,1:T(8,128)S(1)}, f32[30,3,64]{2,0,1:T(8,128)}, u32[]{:S(2)}) copy-start(f32[30,3,64]{2,0,1:T(8,128)} %param.14) | copy-start | bytes 69124
  0.0 1.0 %copy-start.10 = (f32[3,2048]{1,0:T(4,128)S(1)}, f32[3,2048]{1,0:T(4,128)}, u32[]{:S(2)}) copy-start(f32[3,2048]{1,0:T(4,128)} %param.11) | copy-start | bytes 73732
  0.0 1.0 %copy-start.5 = (f32[16,2048]{1,0:T(8,128)S(1)}, f32[16,2048]{1,0:T(8,128)}, u32[]{:S(2)}) copy-start(f32[16,2048]{1,0:T(8,128)} %x_ref.1) | copy-start | bytes 393220
  1.0 0.7 %copy-start.6 = (s32[2,512]{1,0:T(2,128)S(1)}, s32[2,512]{1,0:T(2,128)}, u32[]{:S(2)}) copy-start(s32[2,512]{1,0:T(2,128)} %nlist_ref.1) | copy-start | bytes 12292
  1.0 0.7 %copy-start.8 = (s32[2,16]{1,0:T(2,128)S(1)}, s32[2,16]{1,0:T(2,128)}, u32[]{:S(2)}) copy-start(s32[2,16]{1,0:T(2,128)} %ulist_ref.1) | copy-start | bytes 388
  1.7 1.2 %copy-start = (f32[31,64,64]{2,1,0:T(8,128)S(1)}, f32[31,64,64]{2,1,0:T(8,128)}, u32[]{:S(2)}) copy-start(f32[31,64,64]{2,1,0:T(8,128)} %tr_ref.3) | copy-start | bytes 1523716
  2.9 1.0 %copy-start.2 = (f32[16,64,128]{2,1,0:T(8,128)S(1)}, f32[16,64,128]{2,1,0:T(8,128)}, u32[]{:S(2)}) copy-start(f32[16,64,128]{2,1,0:T(8,128)} %basis_ref.3) | copy-start | bytes 1572868
  3.9 20.1 %copy-start.1 = (f32[31,64,64]{2,1,0:T(8,128)S(1)}, f32[31,64,64]{2,1,0:T(8,128)}, u32[]{:S(2)}) copy-start(f32[31,64,64]{2,1,0:T(8,128)} %tr_ref.3) | copy-start | bytes 1523716
  3.9 20.1 %copy-start.3 = (f32[16,64,128]{2,1,0:T(8,128)S(1)}, f32[16,64,128]{2,1,0:T(8,128)}, u32[]{:S(2)}) copy-start(f32[16,64,128]{2,1,0:T(8,128)} %basis_ref.3) | copy-start | bytes 1572868
  3.9 20.1 %copy-start.4 = (f32[6,64,64]{2,1,0:T(8,128)S(1)}, f32[6,64,64]{2,1,0:T(8,128)}, u32[]{:S(2)}) copy-start(f32[6,64,64]{2,1,0:T(8,128)} %uptr_ref.1) | copy-start | bytes 294916
  24.0 0.7 %copy-start.7 = (s32[2,128]{1,0:T(2,128)S(1)}, s32[2,128]{1,0:T(2,128)}, u32[]{:S(2)}) copy-start(s32[2,128]{1,0:T(2,128)} %far_ref.1) | copy-start | bytes 3076
where the time goes:
time: 50.1 us; the launch traced here: 50 us
  Pallas kernels  45.4 us (91%)
  local copies, waits for them, and re-layouts  4.52 us (9%)
    pallas_call x1, Pallas kernels, per_device(): pl.pallas_call(functools.partial(couple_kernel, n, upper_list.shape[1]),...  25.4 us
    pallas_call x1, Pallas kernels, per_device(): pl.pallas_call(functools.partial(exchange_kernel, n, halo_width), out_sha...  20 us
    unnamed x22, local copies, waits for them, and re-layouts  3.57 us

commit v1 on v0

--- a/solution.py
+++ b/solution.py
@@ -17,7 +17,7 @@
 MESH = pl.DeviceIdType.MESH
 FEATURES = 32
 GROUP = 16
-FAR_GROUP = 16
+FAR_GROUP = 32
 f32 = jnp.float32
 bf16 = jnp.bfloat16
 

time: 50.1 us -> 49.1 us (0.980)
  the two profiles are of different devices: /device:TPU:4 before, /device:TPU:0 now
where the time goes in v1:
time: 49.1 us; the launch traced here: 49.3 us
  Pallas kernels  44.6 us (91%)
  local copies, waits for them, and re-layouts  4.52 us (9%)
    pallas_call x1, Pallas kernels, per_device(): pl.pallas_call(functools.partial(couple_kernel, n, upper_list.shape[1]),...  23.1 us
    pallas_call x1, Pallas kernels, per_device(): pl.pallas_call(functools.partial(exchange_kernel, n, halo_width), out_sha...  21.5 us
    unnamed x22, local copies, waits for them, and re-layouts  3.57 us

profile of v1, /device:TPU:0, one launch (start us, length us, event | category | flops | bytes accessed | tf_op | source)
XLA Modules:
  0.0 49.3 jit_solution(2198623738488550888)
XLA Ops:
  0.0 0.0 copy-start.9
  0.0 0.0 copy-start.10
  0.0 0.0 copy-start.5
  0.0 0.9 %reshape.7 = f32[3,960]{1,0:T(4,128)S(1)} reshape(f32[3,15,64]{2,1,0:T(8,128)} %bitcast.3) | data formatting | bytes 23040 | tf_op jit(solution)/shard_map/reshape | solution.py:534
  0.9 0.0 copy-done.9
  0.9 0.1 reshape.6
  1.0 0.0 copy-done.10
  1.0 0.0 copy-start.6
  1.0 0.0 copy-start.8
  1.0 0.0 copy-done.5
  1.0 0.6 %copy-done.6 = s32[2,512]{1,0:T(2,128)S(1)} copy-done((s32[2,512]{1,0:T(2,128)S(1)}, s32[2,512]{1,0:T(2,128)}, u32[]{:S(2)}) %copy-start.6) | copy-done | bytes 4120
  1.7 0.0 copy-done.8
  1.7 0.0 copy-start
  1.7 1.2 %copy-done = f32[31,64,64]{2,1,0:T(8,128)S(1)} copy-done((f32[31,64,64]{2,1,0:T(8,128)S(1)}, f32[31,64,64]{2,1,0:T(8,128)}, u32[]{:S(2)}) %copy-start) | copy-done | bytes 507928
  2.9 0.0 copy-start.2
  2.9 1.0 %copy-done.2 = f32[16,64,128]{2,1,0:T(8,128)S(1)} copy-done((f32[16,64,128]{2,1,0:T(8,128)S(1)}, f32[16,64,128]{2,1,0:T(8,128)}, u32[]{:S(2)}) %copy-start.2) | copy-done | bytes 524312
  3.9 0.0 copy-start.1
  3.9 0.0 copy-start.3
  3.9 0.0 copy-start.4
  3.9 21.5 %shard_map.100 = (f32[3,16,2048]{2,1,0:T(8,128)S(1)}, f32[3,3,3968]{2,1,0:T(4,128)S(1)}, f32[3,15,16,128]{3,2,1,0:T(8,128)S(1)}, f32[8,24,128]{2,1,0:T(8,128)S(1...) custom-call(f32[16,2048]{1,0:T(8,128)S(1)} %copy-done.5, ...), custom_call_target="tpu_custom_call" | custom-call | tf_op jit(solution)/shard_map/pallas_call | solution.py:537
  25.4 0.0 copy-start.7
  25.5 0.0 copy-done.1
  25.5 0.0 copy-done.3
  25.5 0.0 copy-done.4
  25.5 0.6 %copy-done.7 = s32[2,128]{1,0:T(2,128)S(1)} copy-done((s32[2,128]{1,0:T(2,128)S(1)}, s32[2,128]{1,0:T(2,128)}, u32[]{:S(2)}) %copy-start.7) | copy-done | bytes 1048
  26.1 23.1 %shard_map.101 = f32[16,2048]{1,0:T(8,128)} custom-call(s32[16,128]{1,0:T(8,128)S(1)} %get-tuple-element.12.cols_ref, f32[16,128]{1,0:T(8,128)S(1)} %get-tuple-element.13.wts_ref, s32[2,128]{1,0:T(2,128)S(1)} %copy-done.7, f32[3,16,2048]{2,1,0:T(8,128)S(1)} %get-tuple-element.14.xall, f32[3,3,3968]{2,1,0:T(4,128)S(1)} %get-tuple-element.15.ptsall, ...), custom_call_target="tpu_custom_call" | custom-call | tf_op jit(solution)/shard_map/pallas_call | solution.py:565
  (2 shorter events, 0.0 us)
Async XLA Ops:
  0.0 0.9 %copy-start.9 = (f32[30,3,64]{2,0,1:T(8,128)S(1)}, f32[30,3,64]{2,0,1:T(8,128)}, u32[]{:S(2)}) copy-start(f32[30,3,64]{2,0,1:T(8,128)} %param.14) | copy-start | bytes 69124
  0.0 1.0 %copy-start.10 = (f32[3,2048]{1,0:T(4,128)S(1)}, f32[3,2048]{1,0:T(4,128)}, u32[]{:S(2)}) copy-start(f32[3,2048]{1,0:T(4,128)} %param.11) | copy-start | bytes 73732
  0.0 1.0 %copy-start.5 = (f32[16,2048]{1,0:T(8,128)S(1)}, f32[16,2048]{1,0:T(8,128)}, u32[]{:S(2)}) copy-start(f32[16,2048]{1,0:T(8,128)} %x_ref.1) | copy-start | bytes 393220
  1.0 0.7 %copy-start.6 = (s32[2,512]{1,0:T(2,128)S(1)}, s32[2,512]{1,0:T(2,128)}, u32[]{:S(2)}) copy-start(s32[2,512]{1,0:T(2,128)} %nlist_ref.1) | copy-start | bytes 12292
  1.0 0.7 %copy-start.8 = (s32[2,16]{1,0:T(2,128)S(1)}, s32[2,16]{1,0:T(2,128)}, u32[]{:S(2)}) copy-start(s32[2,16]{1,0:T(2,128)} %ulist_ref.1) | copy-start | bytes 388
  1.7 1.2 %copy-start = (f32[31,64,64]{2,1,0:T(8,128)S(1)}, f32[31,64,64]{2,1,0:T(8,128)}, u32[]{:S(2)}) copy-start(f32[31,64,64]{2,1,0:T(8,128)} %tr_ref.3) | copy-start | bytes 1523716
  2.9 1.0 %copy-start.2 = (f32[16,64,128]{2,1,0:T(8,128)S(1)}, f32[16,64,128]{2,1,0:T(8,128)}, u32[]{:S(2)}) copy-start(f32[16,64,128]{2,1,0:T(8,128)} %basis_ref.3) | copy-start | bytes 1572868
  3.9 21.5 %copy-start.1 = (f32[31,64,64]{2,1,0:T(8,128)S(1)}, f32[31,64,64]{2,1,0:T(8,128)}, u32[]{:S(2)}) copy-start(f32[31,64,64]{2,1,0:T(8,128)} %tr_ref.3) | copy-start | bytes 1523716
  3.9 21.5 %copy-start.3 = (f32[16,64,128]{2,1,0:T(8,128)S(1)}, f32[16,64,128]{2,1,0:T(8,128)}, u32[]{:S(2)}) copy-start(f32[16,64,128]{2,1,0:T(8,128)} %basis_ref.3) | copy-start | bytes 1572868
  3.9 21.5 %copy-start.4 = (f32[6,64,64]{2,1,0:T(8,128)S(1)}, f32[6,64,64]{2,1,0:T(8,128)}, u32[]{:S(2)}) copy-start(f32[6,64,64]{2,1,0:T(8,128)} %uptr_ref.1) | copy-start | bytes 294916
  25.4 0.7 %copy-start.7 = (s32[2,128]{1,0:T(2,128)S(1)}, s32[2,128]{1,0:T(2,128)}, u32[]{:S(2)}) copy-start(s32[2,128]{1,0:T(2,128)} %far_ref.1) | copy-start | bytes 3076
